TPU v7x, 32 devices: a whole 2x2x4 slice. The times are simulated.
32 devices in a mesh: kv: 8 (over y, x, core), tp: 4 (over z).
Axes of the slice: x: 2, y: 2, z: 4, core: 2. Of those that a mesh axis runs over, the one named last changes fastest.
Arguments:
- queries: bfloat16 [2, 6, 16384], P(None, None, 'tp'), may hold values from -12 to 12
- new_kv: bfloat16 [2, 2, 6, 1024], P(None, None, None, 'tp'), may hold values from -9 to 9
- kv_cache: bfloat16 [2, 256, 256, 1024], P(None, 'kv', None, 'tp'), may hold values from -6 to 6
- kv_scales: float32 [2, 256, 8], P(None, 'kv', 'tp'), may hold values from 0.5 to 1.5
- context_lens: int32 [6], replicated, may hold values from 1 to 24320
- block_owner: int32 [256], P('kv'), may hold values from 0 to 6, as said below
- block_index: int32 [256], P('kv'), may hold values from 0 to 94, as said below
- out_weight: bfloat16 [8, 2048, 16384], P('tp', 'kv'), may hold values from -0.046875 to 0.046875
Outputs:
- layer_out: bfloat16 [2, 6, 16384], P(None, None, ('kv', 'tp'))
Inputs may be any that keep to these rules, and one draw needn't show every extreme that they name: `block_owner`: each slot names the request whose block it holds, or 6 for an empty slot. Every block 0 to ceil(context_lens[r] / 256) - 1 of every request is held by exactly one slot. In each group of 32 consecutive slots the used ones come first, and some group uses all of them. `block_index`: an empty slot holds 0.
All inputs are finite; a program needn't handle non-finite values.
Results may differ from a plain program's by a relative error of at most 0.0051.
Values sent between devices are 32-bit elements; how exact they have to be, the bound alone decides.
A program may use at most 192 MiB of HBM per device.

v0:
```python
import math

import jax
import jax.numpy as jnp
from jax import lax
from jax.sharding import PartitionSpec as P

HQ = 128
KVH = 8
HD = 128
R = 6
STEPS = 2
BLOCK = 256


very_negative = -1e30


def joined(value, axis, join):
    pieces = jax.tree.map(lambda part: lax.all_gather(part, axis), value)
    head = jax.tree.map(lambda part: part[0], pieces)
    tail = jax.tree.map(lambda part: part[1:], pieces)
    running, _ = lax.scan(lambda running, piece: (join(running, piece), None), head, tail)
    return running


def group_partials(queries, cache, scales, context_lens, block_owner, block_index):
    heads_per = HQ // KVH
    kv_heads = queries.shape[2] // (heads_per * HD)
    query = (
        queries.reshape(STEPS, R, kv_heads, heads_per, HD)
        .transpose(1, 2, 3, 0, 4)
        .reshape(R, kv_heads, heads_per * STEPS, HD)
    )
    slot_count = cache.shape[1]
    key_rows = cache[0].reshape(slot_count, BLOCK, kv_heads, HD)
    value_rows = cache[1].reshape(slot_count, BLOCK, kv_heads, HD)
    member = block_owner[None, :] == jnp.arange(R, dtype=jnp.int32)[:, None]
    member_slots = member.T
    chosen = jnp.einsum(
        "br,rksd->bksd",
        member_slots.astype(jnp.bfloat16),
        query,
        preferred_element_type=jnp.float32,
    ).astype(jnp.bfloat16)
    factor = 1.0 / math.sqrt(HD)
    scores = jnp.einsum("bksd,btkd->bkst", chosen, key_rows, preferred_element_type=jnp.float32) * (
        scales[0][:, :, None, None] * factor
    )
    positions = block_index[:, None] * BLOCK + jnp.arange(BLOCK, dtype=jnp.int32)[None, :]
    length_cap = (member_slots.astype(jnp.int32) * context_lens[None, :]).sum(1)
    usable = (block_owner < R)[:, None] & (positions < length_cap[:, None])
    masked = jnp.where(usable[:, None, None, :], scores, very_negative)
    block_peak = masked.max(-1)
    peak = jnp.where(member[:, :, None, None], block_peak[None], very_negative).max(1)
    slot_peak = jnp.where(member_slots[:, :, None, None], peak[None], very_negative).max(1)
    softened = jnp.where(usable[:, None, None, :], jnp.exp(masked - slot_peak[..., None]), 0.0)
    slot_total = softened.sum(-1)
    rounded = softened.astype(jnp.bfloat16)
    mixed_values = (
        jnp.einsum("bkst,btkd->bksd", rounded, value_rows, preferred_element_type=jnp.float32)
        * scales[1][:, :, None, None]
    )
    weights = member.astype(jnp.float32)
    total = jnp.einsum("rb,bks->rks", weights, slot_total, precision=lax.Precision.HIGHEST)
    numer = jnp.einsum("rb,bksd->rksd", weights, mixed_values, precision=lax.Precision.HIGHEST)
    return (peak, total, numer)


def combine(earlier, later):
    peak = jnp.maximum(earlier[0], later[0])
    early_weight = jnp.exp(earlier[0] - peak)
    late_weight = jnp.exp(later[0] - peak)
    total = early_weight * earlier[1] + late_weight * later[1]
    numer = early_weight[..., None] * earlier[2] + late_weight[..., None] * later[2]
    return (peak, total, numer)


def finish(peak, total, numer, query, new_keys, new_values):
    factor = 1.0 / math.sqrt(HD)
    fresh_scores = (
        jnp.einsum("rkgsd,trkd->rkgst", query, new_keys, preferred_element_type=jnp.float32)
        * factor
    )
    causal = jnp.arange(STEPS)[None, :] <= jnp.arange(STEPS)[:, None]
    causal_scores = jnp.where(causal, fresh_scores, very_negative)
    peak_all = jnp.maximum(peak, causal_scores.max(-1))
    retain = jnp.exp(peak - peak_all)
    fresh = jnp.where(causal, jnp.exp(fresh_scores - peak_all[..., None]), 0.0)
    denominator = total * retain + fresh.sum(-1)
    numerator = numer * retain[..., None] + jnp.einsum(
        "rkgst,trkd->rkgsd", fresh, new_values.astype(jnp.float32), precision=lax.Precision.HIGHEST
    )
    return (numerator / denominator[..., None]).astype(jnp.bfloat16)


def shards(
    queries, new_kv, kv_cache, kv_scales, context_lens, block_owner, block_index, out_weight
):
    heads_per = HQ // KVH
    kv_heads = queries.shape[2] // (heads_per * HD)
    share = heads_per // lax.axis_size("kv")
    start = lax.axis_index("kv") * share
    peak, total, numer = group_partials(
        queries, kv_cache, kv_scales, context_lens, block_owner, block_index
    )
    peak = peak.reshape(R, kv_heads, heads_per, STEPS)
    total = total.reshape(R, kv_heads, heads_per, STEPS)
    numer = numer.reshape(R, kv_heads, heads_per, STEPS, HD)

    def take_share(values):
        return lax.dynamic_slice_in_dim(values, start, share, 2)

    peak, total, numer = joined((peak, total, numer), "kv", combine)
    peak, total, numer = (take_share(peak), take_share(total), take_share(numer))
    query = queries.reshape(STEPS, R, kv_heads, heads_per, HD)
    query = lax.dynamic_slice_in_dim(query, start, share, 3).transpose(1, 2, 3, 0, 4)
    newer = new_kv.reshape(2, STEPS, R, kv_heads, HD)
    attended = finish(peak, total, numer, query, newer[0], newer[1])
    flat = attended.transpose(3, 0, 1, 2, 4).reshape(STEPS * R, kv_heads * share * HD)
    weight_rows = out_weight.reshape(kv_heads * share * HD, out_weight.shape[2])
    projected = jnp.dot(flat, weight_rows, preferred_element_type=jnp.float32).reshape(
        STEPS, R, out_weight.shape[2]
    )
    return lax.psum_scatter(projected, ("kv", "tp"), scatter_dimension=2, tiled=True).astype(
        jnp.bfloat16
    )


def solution(mesh):
    placed = (
        P(None, None, "tp"),
        P(None, None, None, "tp"),
        P(None, "kv", None, "tp"),
        P(None, "kv", "tp"),
        P(),
        P("kv"),
        P("kv"),
        P("tp", "kv", None),
    )
    return jax.shard_map(
        shards, mesh=mesh, in_specs=placed, out_specs=P(None, None, ("kv", "tp")), check_vma=False
    )
```

profile of v0, /device:TPU:0, one launch (start us, length us, event | category | flops | bytes accessed | tf_op | source)
XLA Modules:
  0.0 353.2 jit_solution(8650988508147219347)
XLA Ops:
  6.5 0.7 broadcast_compare_fusion
  7.2 0.7 iota_compare_fusion.2
  7.9 0.7 iota_compare_fusion.1
  8.6 0.8 select_reduce_fusion.3
  9.3 0.7 broadcast_multiply_fusion
  10.0 0.7 slice_bitcast_fusion.6
  10.7 0.1 copy.177
  10.8 0.1 copy.167
  10.8 1.0 convolution_convert_fusion
  11.9 5.9 %fusion.38 = (bf16[1,32,256,256]{3,2,1,0:T(8,128)(2,1)}, bf16[1,32,256,256]{3,2,1,0:T(8,128)(2,1)}) fusion(bf16[2,32,256,256]{3,2,1,0:T(8,128)(2,1)} %param.12), kind=kLoop, calls=%fused_computation.69 | loop fusion | bytes 16777216 | tf_op jit(solution)/shard_map/slice | solution.py:37
  17.8 6.4 %copy.199 = bf16[1,32,256,256]{2,3,1,0:T(8,128)(2,1)} copy(bf16[1,32,256,256]{3,2,1,0:T(8,128)(2,1)} %get-tuple-element.123) | data formatting | bytes 8388608
  24.2 6.4 %copy.198 = bf16[1,32,256,256]{2,3,1,0:T(8,128)(2,1)} copy(bf16[1,32,256,256]{3,2,1,0:T(8,128)(2,1)} %get-tuple-element.124) | data formatting | bytes 8388608
  30.6 0.1 fusion.22
  30.7 3.3 fusion.4
  34.0 0.1 select_reduce_fusion.1
  34.1 0.1 select_reduce_fusion
  34.3 1.8 convolution_multiply_fusion
  36.1 1.0 fusion.10
  37.2 0.7 copy.179
  37.9 0.0 reduce-scatter.4.cloned.1.call-start
  38.0 0.1 copy.169
  38.1 1.1 fusion.6
  39.2 0.1 copy.172
  39.3 0.2 fusion.20
  39.5 10.7 %all-gather = f32[48,2,16,2]{2,3,1,0:T(2,128)S(1)} all-gather(f32[6,2,16,2]{2,3,1,0:T(2,128)S(1)} %copy.174), channel_id=2, replica_groups=mesh['kv'=8,'tp'=4] {'kv'}, dimensions={0}, use_global_device_ids=true | all-gather | bytes 13824 | tf_op jit(solution)/shard_map/all_gather | solution.py:20
  50.2 0.1 copy.170
  50.4 9.4 %all_gather.9 = f32[8,6,2,16,2]{3,4,2,1,0:T(2,128)S(1)} all-gather(f32[1,6,2,16,2]{3,4,2,1,0:T(2,128)S(1)} %copy.170), channel_id=1, replica_groups=mesh['kv'=8,'tp'=4] {'kv'}, dimensions={0}, use_global_device_ids=true | all-gather | bytes 13824 | tf_op jit(solution)/shard_map/all_gather | solution.py:20
  59.8 0.4 select_reduce_fusion.2
  60.1 6.3 %all-gather.3.cloned.1.call-done = f32[8,6,2,16,2,128]{5,3,4,2,1,0:T(8,128)} async-done(((f32[1,6,2,16,2,128]{5,3,4,2,1,0:T(8,128)}), f32[8,6,2,16,2,128]{5,3,4,2,1,0:T(8,128)}) %all-gather.3.cloned.1.call-update) | async-done | bytes 1572880 | tf_op jit(solution)/shard_map/all_gather | solution.py:20
  66.5 1.0 slice_bitcast_fusion
  67.5 0.1 copy.180
  67.6 0.3 slice-done
  67.9 10.7 %while.14 = (s32[]{:T(128)}, f32[6,2,16,2]{2,3,1,0:T(2,128)S(1)}, f32[6,2,16,2]{2,3,1,0:T(2,128)S(1)}, f32[6,2,16,2,128]{4,3,2,1,0:T(2,128)S(1)}, f32[7,6,2,16,2...) while((s32[]{:T(128)}, f32[6,2,16,2]{2,3,1,0:T(2,128)S(1)}, ...), condition=%wide.region_6.7_spmd, body=%wide.region_5.6_spmd.sunk | while | flops 149762 | bytes 1004645 | solution.py:23
  67.9 0.1 copy.221
  68.1 0.1 copy.222
  68.2 1.2 fusion.45
  69.5 0.1 copy.221
  69.6 0.1 copy.222
  69.8 1.2 fusion.45
  71.0 0.1 copy.221
  71.1 0.1 copy.222
  71.3 1.2 fusion.45
  72.5 0.1 copy.221
  72.7 0.1 copy.222
  72.8 1.2 fusion.45
  74.1 0.1 copy.221
  74.2 0.1 copy.222
  74.4 1.2 fusion.45
  75.6 0.1 copy.221
  75.7 0.1 copy.222
  75.9 1.2 fusion.45
  77.1 0.1 copy.221
  77.3 0.1 copy.222
  77.4 1.2 fusion.45
  78.6 0.1 copy.182
  78.8 0.1 copy.184
  78.9 0.1 fusion.33
  79.0 0.3 fusion.8
  79.3 8.2 %fusion.23 = f32[2,6,16384]{2,1,0:T(8,128)S(1)} fusion(bf16[512,16384,1]{1,0,2:T(8,128)(2,1)} %bitcast.90, bf16[2,6,512]{2,0,1:T(2,128)(2,1)S(1)} %bitcast.99), kind=kOutput, calls=%fused_computation.40 | convolution fusion | flops 201326592 | bytes 17575936 | tf_op jit(solution)/shard_map/dot_general | solution.py:122
  87.5 30.6 %copy.194 = f32[2,6,16384]{0,1,2:T(8,128)} copy(f32[2,6,16384]{2,1,0:T(8,128)S(1)} %fusion.23) | data formatting | bytes 1572864
  118.1 39.5 %reshape.176 = f32[16384,12]{1,0:T(8,128)} reshape(f32[16384,6,2]{2,1,0:T(8,128)} %bitcast.35) | data formatting | bytes 1572864
  157.6 185.9 %reduce-scatter.4.cloned.1.call-done = f32[512,12]{1,0:T(8,128)} async-done(((f32[16384,12]{1,0:T(8,128)}), f32[512,12]{1,0:T(8,128)}) %reduce-scatter.4.cloned.1.call-update) | async-done | bytes 24592
  343.5 1.6 reshape.177
  345.1 1.2 copy.195
  (36 shorter events, 0.6 us)
Async XLA Ops:
  6.5 4.3 %copy-start = (bf16[2,6,4096]{2,0,1:T(2,128)(2,1)S(1)}, bf16[2,6,4096]{2,0,1:T(2,128)(2,1)}, u32[]{:S(2)}) copy-start(bf16[2,6,4096]{2,0,1:T(2,128)(2,1)} %param.10) | copy-start | bytes 294916
  6.5 59.9 %all-gather.3.cloned.1.call-start = ((), (), s32[]{:S(2)}) async-start(), calls=%async_computation.1 | async-start | bytes 1769472 | tf_op jit(solution)/shard_map/all_gather | solution.py:20
  30.7 3.5 %copy-start.1 = (bf16[1,32,256,256]{2,3,1,0:T(8,128)(2,1)S(1)}, bf16[1,32,256,256]{2,3,1,0:T(8,128)(2,1)}, u32[]{:S(2)}) copy-start(bf16[1,32,256,256]{2,3,1,0:T(8,128)(2,1)} %copy.199) | copy-start | bytes 12582916
  34.3 1.8 copy-start.2
  37.2 22.6 %copy-start.3 = (bf16[2,2,6,256]{3,1,2,0:T(2,128)(2,1)S(1)}, bf16[2,2,6,256]{3,1,2,0:T(2,128)(2,1)}, u32[]{:S(2)}) copy-start(bf16[2,2,6,256]{3,1,2,0:T(2,128)(2,1)} %param.11) | copy-start | bytes 36868
  37.9 305.6 %reduce-scatter.4.cloned.1.call-start = ((), (), s32[]{:S(2)}) async-start(), calls=%async_computation.2 | async-start | bytes 8650752
  66.5 1.4 slice-start
Sparse Core Ops, SparseCore 0:
  38.0 28.3 all-gather.2
  157.7 185.7 reduce-scatter.3
where the time goes:
time: 354 us; the launch traced here: 353 us
  waiting for transfers between devices  192 us (54%)
  local copies, waits for them, and re-layouts  96.8 us (27%)
  blocking collectives  20.1 us (6%)
  matrix products  16.1 us (5%)
  other arithmetic  14.1 us (4%)
  between operations  13.6 us (4%)
    unnamed x3, waiting for transfers between devices  186 us
    unnamed x14, local copies, waits for them, and re-layouts  85.8 us
    all_gather x2, blocking collectives, joined(): pieces = jax.tree.map(lambda part: lax.all_gather(part, axis), value)  20.1 us
    dot_general x1, matrix products, shards(): jnp.dot(flat, weight_rows, preferred_element_type=jnp.float32)  8.16 us
    add x7, other arithmetic, combine(): early_weight[..., None] * earlier[2] + late_weight[..., None] * later[2]  8.16 us
  transfers between devices with their start and end apart: 2, of which 2 were waited for; matrix products, arithmetic and copies ran while one was open for 1% of the time, Pallas kernels for 0%

commit v1 on v0

v1 whole, which is shorter than its diff:
```python
import functools
import math

import jax
import jax.numpy as jnp
from jax import lax
from jax.experimental import pallas as pl
from jax.experimental.pallas import tpu as pltpu
from jax.sharding import PartitionSpec as P

HQ = 128
KVH = 8
HD = 128
R = 6
STEPS = 2
BLOCK = 256

very_negative = -1e30
MESH = pl.DeviceIdType.MESH


class Sizes:
    def __init__(self, n_kv, n_tp, kv_heads, slots, width):
        self.n_kv, self.n_tp, self.kv_heads, self.slots = n_kv, n_tp, kv_heads, slots
        self.share = HQ // KVH // n_kv
        self.used_rows = kv_heads * self.share * STEPS
        self.rows = -(-self.used_rows // 8) * 8
        self.all_rows = n_kv * self.rows
        self.depth = kv_heads * HD
        self.stack = R * self.rows
        self.message = self.stack + 8
        self.cols = width // (n_kv * n_tp)
        self.packed = self.cols % 256 == 0
        self.half = self.cols // 2 if self.packed else self.cols
        self.piece = 3 * self.half if self.packed else 2 * self.half
        self.chunk = width // n_kv
        self.pairs = n_kv // 2
        self.load_parts = 4 if slots % 4 == 0 else 1


def flip(index, distance):
    result, bit = index, 1
    while bit <= distance:
        if distance & bit:
            result = result + bit * (1 - 2 * ((index // bit) % 2))
        bit *= 2
    return result


def row_head(z, shape):
    row = lax.broadcasted_iota(jnp.int32, shape, 0) % z.rows
    return row // (z.share * STEPS)


def by_head(z, head, pieces):
    result = pieces[-1]
    for k in range(z.kv_heads - 2, -1, -1):
        result = jnp.where(head == k, pieces[k], result)
    return result


def attend(
    z, lens, owner, number, scales, q_ref, cache, msg, kv_buf, qb, s_buf, m_buf, t_buf, n_buf, peak_buf, sems
):
    part = z.slots // z.load_parts

    def load(which, n):
        piece = pl.ds(n * part, part)
        return pltpu.make_async_copy(cache.at[which, piece], kv_buf.at[which, piece], sems.at[which, n])

    for which in range(2):
        for n in range(z.load_parts):
            load(which, n).start()

    head = row_head(z, (z.all_rows, HD))
    lane = lax.broadcasted_iota(jnp.int32, (z.all_rows, BLOCK), 1)
    factor = 1.0 / math.sqrt(HD)
    for r in range(R):
        rows = q_ref[r].reshape(z.all_rows, HD)
        for k in range(z.kv_heads):
            qb[r, :, k * HD : (k + 1) * HD] = jnp.where(head == k, rows, 0.0).astype(jnp.bfloat16)

    def cap_of(b):
        own = owner[b]
        safe = jnp.minimum(own, R - 1)
        return safe, jnp.where(own < R, lens[safe], 0) - number[b] * BLOCK

    def score(b):
        safe, cap = cap_of(b)
        product = lax.dot_general(
            qb[safe], kv_buf[0, b], (((1,), (1,)), ((), ())), preferred_element_type=jnp.float32
        )
        scale = by_head(
            z, head, [jnp.full((z.all_rows, HD), scales[0, b, k] * factor) for k in range(z.kv_heads)]
        )
        scale = jnp.concatenate([scale] * (BLOCK // HD), 1)
        masked = jnp.where(lane < cap, product * scale, very_negative)
        s_buf[b] = masked
        m_buf[b] = jnp.maximum(masked[:, :HD], masked[:, HD:])

    def mix(b):
        safe, cap = cap_of(b)
        top = peak_buf[safe]
        top = jnp.concatenate([top] * (BLOCK // HD), 1)
        weight = jnp.where(lane < cap, jnp.exp(s_buf[b] - top), 0.0)
        t_buf[b] = weight[:, :HD] + weight[:, HD:]
        product = jnp.dot(weight.astype(jnp.bfloat16), kv_buf[1, b], preferred_element_type=jnp.float32)
        n_buf[b] = by_head(
            z, head, [product[:, k * HD : (k + 1) * HD] * scales[1, b, k] for k in range(z.kv_heads)]
        )

    def sweep(which, step):
        def group(n, carry):
            load(which, n).wait()
            for i in range(part):
                step(n * part + i)
            return carry

        lax.fori_loop(0, z.load_parts, group, 0)

    sweep(0, score)

    def peak_of(r):
        def step(b, top):
            return jnp.maximum(top, m_buf[b] + jnp.where(owner[b] == r, 0.0, 2 * very_negative))

        start = jnp.full((z.all_rows, HD), very_negative, jnp.float32)
        top = lax.fori_loop(0, z.slots, step, start, unroll=8)
        return jnp.broadcast_to(top.max(1, keepdims=True), top.shape)

    for r in range(R):
        peak_buf[r] = peak_of(r)
    sweep(1, mix)

    row = lax.broadcasted_iota(jnp.int32, (z.all_rows, HD), 0) % z.rows
    column = lax.broadcasted_iota(jnp.int32, (z.all_rows, HD), 1)
    peaks = jnp.zeros((z.all_rows, HD), jnp.float32)
    totals = jnp.zeros((z.all_rows, HD), jnp.float32)
    for r in range(R):

        def step(b, sums):
            keep = jnp.where(owner[b] == r, 1.0, 0.0)
            return sums[0] + keep * t_buf[b], sums[1] + keep * n_buf[b]

        zero = jnp.zeros((z.all_rows, HD), jnp.float32)
        total, numer = lax.fori_loop(0, z.slots, step, (zero, zero), unroll=8)
        here = column == r * z.rows + row
        peaks = peaks + jnp.where(here, peak_buf[r], 0.0)
        totals = totals + jnp.where(here, total.sum(1, keepdims=True), 0.0)
        msg[:, r * z.rows : (r + 1) * z.rows, :] = numer.reshape(z.n_kv, z.rows, HD)
    msg[:, z.stack :, :] = jnp.zeros((z.n_kv, 8, HD), jnp.float32)
    msg[:, z.stack : z.stack + 1, :] = peaks.reshape(z.n_kv, z.rows, HD).sum(1, keepdims=True)
    msg[:, z.stack + 1 : z.stack + 2, :] = totals.reshape(z.n_kv, z.rows, HD).sum(1, keepdims=True)


def project(
    z, q_ref, new_ref, w_ref, msg, out_ref,
    w_buf, got, new_x, att, a_rows, sent1, sent2, got1, got2, sums, got3, whole,
    w_sem, m_send, m_recv, send1, recv1, send2, recv2, send3, recv3,
):
    kv, tp = lax.axis_index("kv"), lax.axis_index("tp")
    high, side = kv // 2, kv % 2
    partner = kv + 1 - 2 * side
    order = list(range(z.pairs - 1, -1, -1))

    barrier = pltpu.get_barrier_semaphore()
    for d in range(1, z.n_kv):
        pl.semaphore_signal(barrier, inc=1, device_id=(flip(kv, d), tp), device_id_type=MESH)
    for e in range(1, z.n_tp):
        pl.semaphore_signal(barrier, inc=1, device_id=(kv, (tp + e) % z.n_tp), device_id_type=MESH)

    owners = [2 * flip(high, d) + 1 - side for d in order] + [2 * flip(high, d) + side for d in order]

    def load(n):
        start = pl.multiple_of(owners[n] * z.chunk, z.chunk)
        return pltpu.make_async_copy(w_ref.at[:, :, pl.ds(start, z.chunk)], w_buf.at[n], w_sem.at[n])

    for n in range(z.n_kv):
        load(n).start()

    pl.semaphore_wait(barrier, z.n_kv - 1 + z.n_tp - 1)

    def remote(src, dst, send, recv, target):
        return pltpu.make_async_remote_copy(
            src_ref=src, dst_ref=dst, send_sem=send, recv_sem=recv, device_id=target, device_id_type=MESH
        )

    exchange = []
    for d in range(z.n_kv - 1, 0, -1):
        there = flip(kv, d)
        copy = remote(msg.at[there], got.at[d - 1], m_send.at[d - 1], m_recv.at[d - 1], (there, tp))
        copy.start()
        exchange.append(copy)

    factor = 1.0 / math.sqrt(HD)
    newer = new_ref[...].astype(jnp.float32)
    small = row_head(z, (z.rows, HD))
    for a in range(2):
        for u in range(STEPS):
            for r in range(R):
                pieces = [
                    jnp.broadcast_to(newer[a, u, r : r + 1, k * HD : (k + 1) * HD], (z.rows, HD))
                    for k in range(z.kv_heads)
                ]
                new_x[a, u, r * z.rows : (r + 1) * z.rows, :] = by_head(z, small, pieces)
    query = q_ref[:, kv].reshape(z.stack, HD)
    step_of = lax.broadcasted_iota(jnp.int32, (z.stack, 1), 0) % STEPS
    fresh = [(query * new_x[0, u]).sum(1, keepdims=True) * factor for u in range(STEPS)]
    fresh = [jnp.where(u <= step_of, fresh[u], very_negative) for u in range(STEPS)]
    fresh_top = functools.reduce(jnp.maximum, fresh)
    a_rows[...] = jnp.zeros_like(a_rows)

    for copy in exchange:
        copy.wait()
    spot = lax.broadcasted_iota(jnp.int32, (z.stack, HD), 0) == lax.broadcasted_iota(
        jnp.int32, (z.stack, HD), 1
    )

    def expand(values):
        return jnp.where(spot, values, 0.0).sum(1, keepdims=True)

    stats = [msg[kv, z.stack :, :]] + [got[d, z.stack :, :] for d in range(z.n_kv - 1)]
    peak = functools.reduce(jnp.maximum, [s[0:1] for s in stats])
    weights = [jnp.exp(s[0:1] - peak) for s in stats]
    total = functools.reduce(jnp.add, [w * s[1:2] for w, s in zip(weights, stats)])
    numer = expand(weights[0]) * msg[kv, : z.stack, :]
    for d in range(z.n_kv - 1):
        numer = numer + expand(weights[d + 1]) * got[d, : z.stack, :]
    peak, total = expand(peak), expand(total)
    top = jnp.maximum(peak, fresh_top)
    retain = jnp.exp(peak - top)
    fresh = [jnp.where(u <= step_of, jnp.exp(fresh[u] - top), 0.0) for u in range(STEPS)]
    numer, total = numer * retain, total * retain
    for u in range(STEPS):
        numer = numer + fresh[u] * new_x[1, u]
        total = total + fresh[u]
    att[...] = numer / total

    count = STEPS * R
    for c in range(z.kv_heads * z.share):
        for s in range(STEPS):
            a_rows[0, s * R : (s + 1) * R, c * HD : (c + 1) * HD] = att[
                pl.ds(c * STEPS + s, R, stride=z.rows), :
            ]
    a_rows[1, 0:8, :] = a_rows[0, 0:8, :]
    a_rows[1, 12 : 12 + count - 8, :] = a_rows[0, 8:count, :]
    low = a_rows[0].astype(jnp.bfloat16)
    late = a_rows[1].astype(jnp.bfloat16)
    inner = z.share * HD

    def product(rows, n, start):
        parts = [
            jnp.dot(
                rows[:, k * inner : (k + 1) * inner],
                w_buf[n, k, :, start : start + z.half],
                preferred_element_type=jnp.float32,
            )
            for k in range(z.kv_heads)
        ]
        return functools.reduce(jnp.add, parts)

    def fill(n, t, put):
        first = product(low, n, t * z.cols)
        if z.packed:
            second = product(late, n, t * z.cols + z.half)
            put(slice(0, z.half), first[0:8])
            put(slice(z.half, 2 * z.half), second[0:8])
            put(slice(2 * z.half, 3 * z.half), first[8:16] + second[8:16])
        else:
            put(slice(0, z.half), first[0:8])
            put(slice(z.half, 2 * z.half), first[8:16])

    paired = []
    for n in range(z.pairs):
        load(n).wait()
        for t in range(z.n_tp):

            def put(where, value):
                sent1[n, t, :, where] = value

            fill(n, t, put)
        copy = remote(sent1.at[n], got1.at[n], send1.at[n], recv1.at[n], (partner, tp))
        copy.start()
        paired.append(copy)

    spread = []
    for n, d in enumerate(order):
        load(z.pairs + n).wait()
        paired[n].wait_recv()
        for t in range(z.n_tp):

            def put(where, value):
                sent2[n, t, :, where] = value + got1[n, t, :, where]

            fill(z.pairs + n, t, put)
        if d > 0:
            there = 2 * flip(high, d) + side
            copy = remote(sent2.at[n], got2.at[d - 1], send2.at[d - 1], recv2.at[d - 1], (there, tp))
            copy.start()
            spread.append(copy)

    for copy in spread:
        copy.wait_recv()
    last = []

    def add_up(t):
        value = sent2[z.pairs - 1, t]
        for d in range(z.pairs - 1):
            value = value + got2[d, t]
        return value

    for e in range(1, z.n_tp):
        there = (tp + e) % z.n_tp
        sums[e - 1] = add_up(there)
        copy = remote(sums.at[e - 1], got3.at[e - 1], send3.at[e - 1], recv3.at[e - 1], (kv, there))
        copy.start()
        last.append(copy)
    value = add_up(tp)
    for copy in last:
        copy.wait_recv()
    for e in range(z.n_tp - 1):
        value = value + got3[e]
    if z.packed:
        whole[0:8, : z.half] = value[:, : z.half]
        whole[0:8, z.half :] = value[:, z.half : 2 * z.half]
        whole[8:12, : z.half] = value[0:4, 2 * z.half :]
        whole[8:12, z.half :] = value[4:8, 2 * z.half :]
    else:
        whole[0:8, :] = value[:, : z.half]
        whole[8:16, :] = value[:, z.half :]
    for s in range(STEPS):
        out_ref[s] = whole[s * R : (s + 1) * R, :]
    for copy in paired + spread + last:
        copy.wait_send()


def attend_scratch(z):
    f32, bf16 = jnp.float32, jnp.bfloat16
    tile = (z.slots, z.all_rows, HD)
    return [
        pltpu.VMEM((2, z.slots, BLOCK, z.depth), bf16),
        pltpu.VMEM((R, z.all_rows, z.depth), bf16),
        pltpu.VMEM((z.slots, z.all_rows, BLOCK), f32),
        pltpu.VMEM(tile, f32),
        pltpu.VMEM(tile, f32),
        pltpu.VMEM(tile, f32),
        pltpu.VMEM((R, z.all_rows, HD), f32),
        pltpu.SemaphoreType.DMA((2, z.load_parts)),
    ]


def project_scratch(z):
    f32, bf16 = jnp.float32, jnp.bfloat16
    dma = pltpu.SemaphoreType.DMA
    rest, others = max(z.pairs - 1, 1), max(z.n_tp - 1, 1)
    part = (z.n_tp, 8, z.piece)
    return [
        pltpu.VMEM((z.n_kv, z.kv_heads, z.share * HD, z.chunk), bf16),
        pltpu.VMEM((z.n_kv - 1, z.message, HD), f32),
        pltpu.VMEM((2, STEPS, z.stack, HD), f32),
        pltpu.VMEM((z.stack, HD), f32),
        pltpu.VMEM((2, 16, z.kv_heads * z.share * HD), f32),
        pltpu.VMEM((z.pairs, *part), f32),
        pltpu.VMEM((z.pairs, *part), f32),
        pltpu.VMEM((z.pairs, *part), f32),
        pltpu.VMEM((rest, *part), f32),
        pltpu.VMEM((others, 8, z.piece), f32),
        pltpu.VMEM((others, 8, z.piece), f32),
        pltpu.VMEM((16, z.cols), f32),
        dma((z.n_kv,)),
        dma((z.n_kv - 1,)),
        dma((z.n_kv - 1,)),
        dma((z.pairs,)),
        dma((z.pairs,)),
        dma((rest,)),
        dma((rest,)),
        dma((others,)),
        dma((others,)),
    ]


def spaces(*names):
    kinds = {"s": pltpu.SMEM, "v": pltpu.VMEM, "h": pl.ANY}
    return [pl.BlockSpec(memory_space=kinds[name]) for name in names]


def shards(
    queries, new_kv, kv_cache, kv_scales, context_lens, block_owner, block_index, out_weight
):
    n_kv, n_tp = lax.axis_size("kv"), lax.axis_size("tp")
    kv_heads = kv_cache.shape[3] // HD
    z = Sizes(n_kv, n_tp, kv_heads, kv_cache.shape[1], out_weight.shape[2])
    query = (
        queries.reshape(STEPS, R, kv_heads, n_kv, z.share, HD)
        .transpose(1, 3, 2, 4, 0, 5)
        .reshape(R, n_kv, z.used_rows, HD)
        .astype(jnp.float32)
    )
    query = jnp.pad(query, ((0, 0), (0, 0), (0, z.rows - z.used_rows), (0, 0)))
    msg = pl.pallas_call(
        functools.partial(attend, z),
        out_shape=jax.ShapeDtypeStruct((n_kv, z.message, HD), jnp.float32),
        in_specs=spaces(*"ssssvh"),
        out_specs=spaces("v")[0],
        scratch_shapes=attend_scratch(z),
        compiler_params=pltpu.CompilerParams(vmem_limit_bytes=56 * 2**20),
        name="attend",
    )(context_lens, block_owner, block_index, kv_scales, query, kv_cache)
    out = pl.pallas_call(
        functools.partial(project, z),
        out_shape=jax.ShapeDtypeStruct((STEPS, R, z.cols), jnp.float32),
        in_specs=spaces(*"vvhv"),
        out_specs=spaces("v")[0],
        scratch_shapes=project_scratch(z),
        compiler_params=pltpu.CompilerParams(
            vmem_limit_bytes=56 * 2**20, collective_id=0, has_side_effects=True
        ),
        name="project",
    )(query, new_kv, out_weight, msg)
    return out.astype(jnp.bfloat16)


def solution(mesh):
    placed = (
        P(None, None, "tp"),
        P(None, None, None, "tp"),
        P(None, "kv", None, "tp"),
        P(None, "kv", "tp"),
        P(),
        P("kv"),
        P("kv"),
        P("tp", "kv", None),
    )
    return jax.shard_map(
        shards, mesh=mesh, in_specs=placed, out_specs=P(None, None, ("kv", "tp")), check_vma=False
    )
```

time: 354 us -> 39.4 us (0.11)
  waiting for transfers between devices: 192 us -> 0 us
  local copies, waits for them, and re-layouts: 96.8 us -> 5.14 us
  Pallas kernels: 0 us -> 33.2 us
  blocking collectives: 20.1 us -> 0 us
  matrix products: 16.1 us -> 0 us
  between operations: 13.6 us -> 0.02 us
  other arithmetic: 14.1 us -> 0.76 us
    unnamed x3 -> x0, waiting for transfers between devices: 186 us -> none
    unnamed x14 -> x2, local copies, waits for them, and re-layouts: 85.8 us -> 2.68 us
    pallas_call x0 -> x2, Pallas kernels: none -> 33.2 us  [the longest x1 24.5 us: shards(): pl.pallas_call(functools.partial(project, z), out_shape=jax.ShapeDtypeStr...]
    all_gather x2 -> x0, blocking collectives: 20.1 us -> none  [joined(): pieces = jax.tree.map(lambda part: lax.all_gather(part, axis), value)]
    dot_general x8 -> x0, matrix products: 16.1 us -> none  [the longest x1 8.16 us: shards(): jnp.dot(flat, weight_rows, preferred_element_type=jnp.float32)]
    add x15 -> x0, other arithmetic: 8.47 us -> none  [the longest x7 8.16 us: combine(): early_weight[..., None] * earlier[2] + late_weight[..., None] * later[2]]
    all_gather x1 -> x0, waiting for transfers between devices: 6.35 us -> none  [joined(): pieces = jax.tree.map(lambda part: lax.all_gather(part, axis), value)]
    slice x6 -> x0, local copies, waits for them, and re-layouts: 6.23 us -> none  [the longest x1 5.95 us: group_partials(): value_rows = cache[1].reshape(slot_count, BLOCK, kv_heads, HD)]
  transfers between devices with their start and end apart: 2 -> 0, of which waited for: 2 -> 0; matrix products, arithmetic and copies ran while one was open for 1% -> 0% of each run, Pallas kernels for 0% -> 0%
where the time goes in v1:
time: 39.4 us; the launch traced here: 39.1 us
  Pallas kernels  33.2 us (84%)
  local copies, waits for them, and re-layouts  5.14 us (13%)
  other arithmetic  0.76 us (2%)
    pallas_call x1, Pallas kernels, shards(): pl.pallas_call(functools.partial(project, z), out_shape=jax.ShapeDtypeStr...  24.5 us
    pallas_call x1, Pallas kernels, shards(): pl.pallas_call(functools.partial(attend, z), out_shape=jax.ShapeDtypeStru...  8.66 us
    unnamed x2, local copies, waits for them, and re-layouts  2.68 us
    convert_element_type x2, local copies, waits for them, and re-layouts, shards(): query = queries.reshape(STEPS, R, kv_heads, n_kv, z.share, HD).transpose(...  1.84 us

profile of v1, /device:TPU:0, one launch (start us, length us, event | category | flops | bytes accessed | tf_op | source)
XLA Modules:
  0.0 39.1 jit_solution(9076288410479987758)
XLA Ops:
  0.0 1.3 %copy.15.new_ref = bf16[2,2,6,256]{3,2,1,0:T(8,128)(2,1)} copy(bf16[2,2,6,256]{3,1,2,0:T(2,128)(2,1)} %param.9) | data formatting | bytes 24576 | tf_op args[1]
  1.3 1.4 %copy.14.scales = f32[2,32,2]{2,1,0:T(8,128)} copy(f32[2,32,2]{1,2,0:T(2,128)} %param.11) | data formatting | bytes 1024 | tf_op args[3]
  2.7 1.0 %reshape.7 = f32[2,6,2,8,2,128]{5,4,3,2,0,1:T(2,128)S(1)} reshape(bf16[2,6,4096]{2,0,1:T(2,128)(2,1)} %param.8) | data formatting | bytes 294912 | tf_op jit(solution)/shard_map/convert_element_type | solution.py:397
  3.7 0.8 %copy.13 = f32[2,6,2,8,2,128]{5,0,4,2,3,1:T(2,128)} copy(f32[2,6,2,8,2,128]{5,4,3,2,0,1:T(2,128)S(1)} %reshape.7) | data formatting | bytes 393216 | tf_op jit(solution)/shard_map/convert_element_type | solution.py:397
  4.5 8.7 %attend.1.msg = f32[8,56,128]{2,1,0:T(8,128)} custom-call(s32[6]{0:T(128)} %lens.1, s32[32]{0:T(128)} %owner.1, s32[32]{0:T(128)} %number.1, f32[2,32,2]{2,1,0:T(8,128)} %copy.14.scales, f32[6,8,8,128]{3,2,1,0:T(8,128)} %bitcast.5, bf16[2,32,256,256]{3,2,1,0:T(8,128)(2,1)} %cache.1), custom_call_target="tpu_custom_call" | custom-call | tf_op jit(solution)/shard_map/attend/pallas_call | solution.py:400
  13.2 24.5 %project.1 = f32[2,6,512]{2,1,0:T(8,128)} custom-call(f32[6,8,8,128]{3,2,1,0:T(8,128)} %bitcast.6, bf16[2,2,6,256]{3,2,1,0:T(8,128)(2,1)} %copy.15.new_ref, bf16[2,256,16384]{2,1,0:T(8,128)(2,1)} %w_ref.1, f32[8,56,128]{2,1,0:T(8,128)} %attend.1.msg), custom_call_target="tpu_custom_call" | custom-call | tf_op jit(solution)/shard_map/project/pallas_call | solution.py:409
  37.7 0.8 %convert_element_type.16 = bf16[2,6,512]{2,1,0:T(8,128)(2,1)S(1)} convert(f32[2,6,512]{2,1,0:T(8,128)} %project.1) | non-fusion elementwise | flops 6144 | bytes 36864 | tf_op jit(solution)/shard_map/convert_element_type | solution.py:420
  38.5 0.6 %copy.16 = bf16[2,6,512]{2,0,1:T(2,128)(2,1)} copy(bf16[2,6,512]{2,1,0:T(8,128)(2,1)S(1)} %convert_element_type.16) | data formatting | bytes 24576 | tf_op jit(solution)/shard_map/convert_element_type | solution.py:420

commit v2 on v1

v2 whole, which is shorter than its diff:
```python
import functools
import math

import jax
import jax.numpy as jnp
from jax import lax
from jax.experimental import pallas as pl
from jax.experimental.pallas import tpu as pltpu
from jax.sharding import PartitionSpec as P

HQ = 128
KVH = 8
HD = 128
R = 6
STEPS = 2
BLOCK = 256

very_negative = -1e30
MESH = pl.DeviceIdType.MESH


class Sizes:
    def __init__(self, n_kv, n_tp, kv_heads, slots, width):
        self.n_kv, self.n_tp, self.kv_heads, self.slots = n_kv, n_tp, kv_heads, slots
        self.share = HQ // KVH // n_kv
        self.used_rows = kv_heads * self.share * STEPS
        self.rows = -(-self.used_rows // 8) * 8
        self.all_rows = n_kv * self.rows
        self.depth = kv_heads * HD
        self.stack = R * self.rows
        self.message = self.stack + 8
        self.cols = width // (n_kv * n_tp)
        self.packed = self.cols % 256 == 0
        self.half = self.cols // 2 if self.packed else self.cols
        self.piece = 3 * self.half if self.packed else 2 * self.half
        self.width = width
        self.inner = self.share * HD
        self.pairs = n_kv // 2
        self.load_parts = 4 if slots % 4 == 0 else 1


def flip(index, distance):
    result, bit = index, 1
    while bit <= distance:
        if distance & bit:
            result = result + bit * (1 - 2 * ((index // bit) % 2))
        bit *= 2
    return result


def row_head(z, shape):
    row = lax.broadcasted_iota(jnp.int32, shape, 0) % z.rows
    return row // (z.share * STEPS)


def by_head(z, head, pieces):
    result = pieces[-1]
    for k in range(z.kv_heads - 2, -1, -1):
        result = jnp.where(head == k, pieces[k], result)
    return result


def attend(
    z, lens, owner, number, scales, queries, msg, q_rows, kv_buf, qb, s_buf, m_buf, t_buf, n_buf, peak_buf, load, between
):
    part = z.slots // z.load_parts
    head = row_head(z, (z.all_rows, HD))
    lane = lax.broadcasted_iota(jnp.int32, (z.all_rows, BLOCK), 1)
    factor = 1.0 / math.sqrt(HD)
    if z.used_rows < z.rows:
        q_rows[...] = jnp.zeros_like(q_rows)
    for r in range(R):
        flat = queries[r].astype(jnp.float32)
        for k in range(z.kv_heads):
            for j in range(z.n_kv):
                for g in range(z.share):
                    h = (k * z.n_kv + j) * z.share + g
                    row = (k * z.share + g) * STEPS
                    q_rows[r, j, row : row + STEPS, :] = flat[:, h * HD : (h + 1) * HD]
    for r in range(R):
        rows = q_rows[r].reshape(z.all_rows, HD)
        for k in range(z.kv_heads):
            qb[r, :, k * HD : (k + 1) * HD] = jnp.where(head == k, rows, 0.0).astype(jnp.bfloat16)
    blank = jnp.zeros((z.all_rows, HD), jnp.float32)
    m_buf[z.slots] = blank + very_negative
    t_buf[z.slots] = blank
    n_buf[z.slots] = blank

    def cap_of(b):
        own = owner[b]
        safe = jnp.minimum(own, R - 1)
        return safe, jnp.where(own < R, lens[safe], 0) - number[b] * BLOCK

    def score(b, before):
        safe, cap = cap_of(b)
        product = lax.dot_general(
            qb[safe], kv_buf[0, b], (((1,), (1,)), ((), ())), preferred_element_type=jnp.float32
        )
        scale = by_head(z, head, [jnp.full((z.all_rows, HD), scales[0, k, b] * factor) for k in range(z.kv_heads)])
        scale = jnp.concatenate([scale] * (BLOCK // HD), 1)
        masked = jnp.where(lane < cap, product * scale, very_negative)
        s_buf[b] = masked
        m_buf[b] = jnp.maximum(jnp.maximum(masked[:, :HD], masked[:, HD:]), m_buf[before])

    def mix(b, before):
        safe, cap = cap_of(b)
        top = peak_buf[safe]
        top = jnp.concatenate([top] * (BLOCK // HD), 1)
        weight = jnp.where(lane < cap, jnp.exp(s_buf[b] - top), 0.0)
        t_buf[b] = weight[:, :HD] + weight[:, HD:] + t_buf[before]
        product = jnp.dot(weight.astype(jnp.bfloat16), kv_buf[1, b], preferred_element_type=jnp.float32)
        mixed = by_head(z, head, [product[:, k * HD : (k + 1) * HD] * scales[1, k, b] for k in range(z.kv_heads)])
        n_buf[b] = mixed + n_buf[before]

    def sweep(which, step):
        def group(n, last):
            load(which, n).wait()
            last = list(last)
            for i in range(part):
                b = n * part + i
                own = owner[b]
                before = jnp.int32(z.slots)
                for r in range(R):
                    before = jnp.where(own == r, last[r], before)
                step(b, before)
                last = [jnp.where(own == r, b, last[r]) for r in range(R)]
            return tuple(last)

        return lax.fori_loop(0, z.load_parts, group, (jnp.int32(z.slots),) * R)

    last = sweep(0, score)
    between()
    for r in range(R):
        peak_buf[r] = jnp.broadcast_to(m_buf[last[r]].max(1, keepdims=True), (z.all_rows, HD))
    last = sweep(1, mix)

    row = lax.broadcasted_iota(jnp.int32, (z.all_rows, HD), 0) % z.rows
    column = lax.broadcasted_iota(jnp.int32, (z.all_rows, HD), 1)
    peaks, totals = blank, blank
    for r in range(R):
        here = column == r * z.rows + row
        peaks = peaks + jnp.where(here, peak_buf[r], 0.0)
        totals = totals + jnp.where(here, t_buf[last[r]].sum(1, keepdims=True), 0.0)
        msg[:, r * z.rows : (r + 1) * z.rows, :] = n_buf[last[r]].reshape(z.n_kv, z.rows, HD)
    msg[:, z.stack :, :] = jnp.zeros((z.n_kv, 8, HD), jnp.float32)
    msg[:, z.stack : z.stack + 1, :] = peaks.reshape(z.n_kv, z.rows, HD).sum(1, keepdims=True)
    msg[:, z.stack + 1 : z.stack + 2, :] = totals.reshape(z.n_kv, z.rows, HD).sum(1, keepdims=True)


def layer(
    z, lens, owner, number, scales, queries, new_ref, cache, w_ref, out_ref,
    kv_buf, q_rows, qb, s_buf, m_buf, t_buf, n_buf, peak_buf, msg,
    w_buf, got, new_x, att, a_rows, sent1, got1, sent2, got2, sums, got3, whole,
    c_sem, w_sem, m_send, m_recv, send1, recv1, send2, recv2, send3, recv3,
):
    kv, tp = lax.axis_index("kv"), lax.axis_index("tp")
    high, side = kv // 2, kv % 2
    partner = kv + 1 - 2 * side
    order = list(range(z.pairs - 1, -1, -1))
    turns = [(e + 1) % z.n_tp for e in range(z.n_tp)]
    part = z.slots // z.load_parts

    def load(which, n):
        piece = pl.ds(n * part, part)
        return pltpu.make_async_copy(cache.at[which, piece], kv_buf.at[which, piece], c_sem.at[which, n])

    for which in range(2):
        for n in range(z.load_parts):
            load(which, n).start()

    barrier = pltpu.get_barrier_semaphore()
    for d in range(1, z.n_kv):
        pl.semaphore_signal(barrier, inc=1, device_id=(flip(kv, d), tp), device_id_type=MESH)
    for e in range(1, z.n_tp):
        pl.semaphore_signal(barrier, inc=1, device_id=(kv, (tp + e) % z.n_tp), device_id_type=MESH)

    block = z.inner // 4

    def load_weight(k, n):
        piece = pl.ds(n * block, block)
        return pltpu.make_async_copy(w_ref.at[k, piece], w_buf.at[k, piece], w_sem.at[k, n])

    def load_weights():
        for k in range(z.kv_heads):
            for n in range(4):
                load_weight(k, n).start()

    attend(
        z, lens, owner, number, scales, queries, msg, q_rows, kv_buf, qb, s_buf, m_buf, t_buf, n_buf, peak_buf, load, load_weights
    )
    pl.semaphore_wait(barrier, z.n_kv - 1 + z.n_tp - 1)

    def remote(src, dst, send, recv, target):
        return pltpu.make_async_remote_copy(
            src_ref=src, dst_ref=dst, send_sem=send, recv_sem=recv, device_id=target, device_id_type=MESH
        )

    exchange = []
    for d in range(z.n_kv - 1, 0, -1):
        there = flip(kv, d)
        copy = remote(msg.at[there], got.at[d - 1], m_send.at[d - 1], m_recv.at[d - 1], (there, tp))
        copy.start()
        exchange.append(copy)

    factor = 1.0 / math.sqrt(HD)
    newer = new_ref[...].astype(jnp.float32)
    small = row_head(z, (z.rows, HD))
    for a in range(2):
        for u in range(STEPS):
            for r in range(R):
                pieces = [
                    jnp.broadcast_to(newer[a, r, u : u + 1, k * HD : (k + 1) * HD], (z.rows, HD))
                    for k in range(z.kv_heads)
                ]
                new_x[a, u, r * z.rows : (r + 1) * z.rows, :] = by_head(z, small, pieces)
    query = q_rows[:, kv].reshape(z.stack, HD)
    step_of = lax.broadcasted_iota(jnp.int32, (z.stack, 1), 0) % STEPS
    fresh = [(query * new_x[0, u]).sum(1, keepdims=True) * factor for u in range(STEPS)]
    fresh = [jnp.where(u <= step_of, fresh[u], very_negative) for u in range(STEPS)]
    fresh_top = functools.reduce(jnp.maximum, fresh)
    a_rows[...] = jnp.zeros_like(a_rows)

    for copy in exchange:
        copy.wait_recv()
    spot = lax.broadcasted_iota(jnp.int32, (z.stack, HD), 0) == lax.broadcasted_iota(
        jnp.int32, (z.stack, HD), 1
    )

    def expand(values):
        return jnp.where(spot, values, 0.0).sum(1, keepdims=True)

    stats = [msg[kv, z.stack :, :]] + [got[d, z.stack :, :] for d in range(z.n_kv - 1)]
    peak = functools.reduce(jnp.maximum, [s[0:1] for s in stats])
    weights = [jnp.exp(s[0:1] - peak) for s in stats]
    total = functools.reduce(jnp.add, [w * s[1:2] for w, s in zip(weights, stats)])
    numer = expand(weights[0]) * msg[kv, : z.stack, :]
    for d in range(z.n_kv - 1):
        numer = numer + expand(weights[d + 1]) * got[d, : z.stack, :]
    peak, total = expand(peak), expand(total)
    top = jnp.maximum(peak, fresh_top)
    retain = jnp.exp(peak - top)
    fresh = [jnp.where(u <= step_of, jnp.exp(fresh[u] - top), 0.0) for u in range(STEPS)]
    numer, total = numer * retain, total * retain
    for u in range(STEPS):
        numer = numer + fresh[u] * new_x[1, u]
        total = total + fresh[u]
    att[...] = numer / total

    count = STEPS * R
    for c in range(z.kv_heads * z.share):
        for s in range(STEPS):
            a_rows[0, s * R : (s + 1) * R, c * HD : (c + 1) * HD] = att[
                pl.ds(c * STEPS + s, R, stride=z.rows), :
            ]
    a_rows[1, 0:8, :] = a_rows[0, 0:8, :]
    a_rows[1, 12 : 12 + count - 8, :] = a_rows[0, 8:count, :]
    low = a_rows[0].astype(jnp.bfloat16)
    late = a_rows[1].astype(jnp.bfloat16)

    for k in range(z.kv_heads):
        for n in range(4):
            load_weight(k, n).wait()

    def product(rows, start):
        columns = pl.ds(pl.multiple_of(start, z.half), z.half)
        parts = [
            jnp.dot(
                rows[:, k * z.inner : (k + 1) * z.inner],
                w_buf[k, :, columns],
                preferred_element_type=jnp.float32,
            )
            for k in range(z.kv_heads)
        ]
        return functools.reduce(jnp.add, parts)

    def fill(j, t, put):
        start = (j * z.n_tp + t) * z.cols
        first = product(low, start)
        if z.packed:
            second = product(late, start + z.half)
            put(slice(0, z.half), first[0:8])
            put(slice(z.half, 2 * z.half), second[0:8])
            put(slice(2 * z.half, 3 * z.half), first[8:16] + second[8:16])
        else:
            put(slice(0, z.half), first[0:8])
            put(slice(z.half, 2 * z.half), first[8:16])

    paired = []
    for i, e in enumerate(turns):
        for n, d in enumerate(order):

            def put(where, value):
                sent1[i, n, :, where] = value

            fill(2 * flip(high, d) + 1 - side, (tp + e) % z.n_tp, put)
        copy = remote(sent1.at[i], got1.at[i], send1.at[i], recv1.at[i], (partner, tp))
        copy.start()
        paired.append(copy)

    spread = []
    for i, e in enumerate(turns):
        paired[i].wait_recv()
        arriving = []
        for n, d in enumerate(order):

            def put(where, value):
                sent2[i, n, :, where] = value + got1[i, n, :, where]

            there = 2 * flip(high, d) + side
            fill(there, (tp + e) % z.n_tp, put)
            if d > 0:
                copy = remote(
                    sent2.at[i, n], got2.at[i, d - 1], send2.at[i, d - 1], recv2.at[i, d - 1], (there, tp)
                )
                copy.start()
                arriving.append(copy)
        spread.append(arriving)

    last = []
    for i, e in enumerate(turns):
        for copy in spread[i]:
            copy.wait_recv()
        value = sent2[i, z.pairs - 1]
        for d in range(z.pairs - 1):
            value = value + got2[i, d]
        if e > 0:
            sums[e - 1] = value
            there = (tp + e) % z.n_tp
            copy = remote(sums.at[e - 1], got3.at[e - 1], send3.at[e - 1], recv3.at[e - 1], (kv, there))
            copy.start()
            last.append(copy)
    for copy in last:
        copy.wait_recv()
    for e in range(z.n_tp - 1):
        value = value + got3[e]
    if z.packed:
        whole[0:8, : z.half] = value[:, : z.half]
        whole[0:8, z.half :] = value[:, z.half : 2 * z.half]
        whole[8:12, : z.half] = value[0:4, 2 * z.half :]
        whole[8:12, z.half :] = value[4:8, 2 * z.half :]
    else:
        whole[0:8, :] = value[:, : z.half]
        whole[8:16, :] = value[:, z.half :]
    for r in range(R):
        for s in range(STEPS):
            out_ref[r, s : s + 1, :] = whole[s * R + r : s * R + r + 1, :]
    for copy in exchange:
        copy.wait_send()
    for copy in paired + sum(spread, []) + last:
        copy.wait_send()


def scratch(z):
    f32, bf16 = jnp.float32, jnp.bfloat16
    dma = pltpu.SemaphoreType.DMA
    tile = (z.slots + 1, z.all_rows, HD)
    rest, others = max(z.pairs - 1, 1), max(z.n_tp - 1, 1)
    part = (8, z.piece)
    return [
        pltpu.VMEM((2, z.slots, BLOCK, z.depth), bf16),
        pltpu.VMEM((R, z.n_kv, z.rows, HD), f32),
        pltpu.VMEM((R, z.all_rows, z.depth), bf16),
        pltpu.VMEM((z.slots, z.all_rows, BLOCK), f32),
        pltpu.VMEM(tile, f32),
        pltpu.VMEM(tile, f32),
        pltpu.VMEM(tile, f32),
        pltpu.VMEM((R, z.all_rows, HD), f32),
        pltpu.VMEM((z.n_kv, z.message, HD), f32),
        pltpu.VMEM((z.kv_heads, z.inner, z.width), bf16),
        pltpu.VMEM((z.n_kv - 1, z.message, HD), f32),
        pltpu.VMEM((2, STEPS, z.stack, HD), f32),
        pltpu.VMEM((z.stack, HD), f32),
        pltpu.VMEM((2, 16, z.kv_heads * z.inner), f32),
        pltpu.VMEM((z.n_tp, z.pairs, *part), f32),
        pltpu.VMEM((z.n_tp, z.pairs, *part), f32),
        pltpu.VMEM((z.n_tp, z.pairs, *part), f32),
        pltpu.VMEM((z.n_tp, rest, *part), f32),
        pltpu.VMEM((others, *part), f32),
        pltpu.VMEM((others, *part), f32),
        pltpu.VMEM((16, z.cols), f32),
        dma((2, z.load_parts)),
        dma((z.kv_heads, 4)),
        dma((z.n_kv - 1,)),
        dma((z.n_kv - 1,)),
        dma((z.n_tp,)),
        dma((z.n_tp,)),
        dma((z.n_tp, rest)),
        dma((z.n_tp, rest)),
        dma((others,)),
        dma((others,)),
    ]


def spaces(*names):
    kinds = {"s": pltpu.SMEM, "v": pltpu.VMEM, "h": pl.ANY}
    return [pl.BlockSpec(memory_space=kinds[name]) for name in names]


def shards(
    queries, new_kv, kv_cache, kv_scales, context_lens, block_owner, block_index, out_weight
):
    n_kv, n_tp = lax.axis_size("kv"), lax.axis_size("tp")
    kv_heads = kv_cache.shape[3] // HD
    z = Sizes(n_kv, n_tp, kv_heads, kv_cache.shape[1], out_weight.shape[2])
    out = pl.pallas_call(
        functools.partial(layer, z),
        out_shape=jax.ShapeDtypeStruct((R, STEPS, z.cols), jnp.float32),
        in_specs=spaces(*"ssssvvhh"),
        out_specs=spaces("v")[0],
        scratch_shapes=scratch(z),
        compiler_params=pltpu.CompilerParams(
            vmem_limit_bytes=56 * 2**20, collective_id=0, has_side_effects=True
        ),
        name="layer",
    )(
        context_lens,
        block_owner,
        block_index,
        kv_scales.transpose(0, 2, 1),
        queries.transpose(1, 0, 2),
        new_kv.transpose(0, 2, 1, 3),
        kv_cache,
        out_weight,
    )
    return out.transpose(1, 0, 2).astype(jnp.bfloat16)


def solution(mesh):
    placed = (
        P(None, None, "tp"),
        P(None, None, None, "tp"),
        P(None, "kv", None, "tp"),
        P(None, "kv", "tp"),
        P(),
        P("kv"),
        P("kv"),
        P("tp", "kv", None),
    )
    return jax.shard_map(
        shards, mesh=mesh, in_specs=placed, out_specs=P(None, None, ("kv", "tp")), check_vma=False
    )
```

time: 39.4 us -> 26.3 us (0.67)
  Pallas kernels: 33.2 us -> 24.8 us
  local copies, waits for them, and re-layouts: 5.14 us -> 0 us
  other arithmetic: 0.76 us -> 1.35 us
    pallas_call x2 -> x1, Pallas kernels: 33.2 us -> 24.8 us  [shards(): pl.pallas_call(functools.partial(layer, z), out_shape=jax.ShapeDtypeStruc...]
    unnamed x2 -> x0, local copies, waits for them, and re-layouts: 2.68 us -> none
    convert_element_type x3 -> x0, local copies, waits for them, and re-layouts: 2.45 us -> none  [the longest x2 1.84 us: shards(): query = queries.reshape(STEPS, R, kv_heads, n_kv, z.share, HD).transpose(...]
    convert_element_type x1, other arithmetic: 0.76 us -> 1.35 us  [shards(): return out.transpose(1, 0, 2).astype(jnp.bfloat16)]
where the time goes in v2:
time: 26.3 us; the launch traced here: 26.1 us
  Pallas kernels  24.8 us (94%)
  other arithmetic  1.35 us (5%)
    pallas_call x1, Pallas kernels, shards(): pl.pallas_call(functools.partial(layer, z), out_shape=jax.ShapeDtypeStruc...  24.8 us
    convert_element_type x1, other arithmetic, shards(): return out.transpose(1, 0, 2).astype(jnp.bfloat16)  1.35 us

profile of v2, /device:TPU:0, one launch (start us, length us, event | category | flops | bytes accessed | tf_op | source)
XLA Modules:
  0.0 26.1 jit_solution(1310819635152871171)
XLA Ops:
  0.0 24.8 %layer.1 = f32[6,2,512]{2,1,0:T(2,128)} custom-call(s32[6]{0:T(128)} %lens.1, s32[32]{0:T(128)} %owner.1, s32[32]{0:T(128)} %number.1, f32[2,2,32]{2,1,0:T(2,128)} %bitcast.7, bf16[6,2,4096]{2,1,0:T(2,128)(2,1)} %bitcast.5, bf16[2,6,2,256]{3,2,1,0:T(2,128)(2,1)} %bitcast.6, bf16[2,32,256,256]{3,2,1,0:T(8,128)(2,1)} %cache.1, bf16[2,256,16384]{2,1,0:T(8,128)(2,1)} %w_ref.1), custom_call_target="tpu_custom_call" | custom-call | tf_op jit(solution)/shard_map/layer/pallas_call | solution.py:405
  24.8 1.3 %convert_bitcast_fusion = bf16[2,6,512]{2,0,1:T(2,128)(2,1)} fusion(f32[6,2,512]{2,1,0:T(2,128)} %layer.1), kind=kLoop, calls=%fused_computation | loop fusion | flops 6144 | bytes 36864 | tf_op jit(solution)/shard_map/convert_element_type | solution.py:425

commit v3 on v2

--- a/solution.py
+++ b/solution.py
@@ -36,6 +36,7 @@
         self.width = width
         self.inner = self.share * HD
         self.pairs = n_kv // 2
+        self.groups = [1] * n_tp
         self.load_parts = 4 if slots % 4 == 0 else 1
 
 
@@ -61,7 +62,7 @@
 
 
 def attend(
-    z, lens, owner, number, scales, queries, msg, q_rows, kv_buf, qb, s_buf, m_buf, t_buf, n_buf, peak_buf, load, between
+    z, lens, owner, number, scales, queries, msg, q_rows, kv_buf, qb, s_buf, m_buf, t_buf, n_buf, peak_buf, load, between, newest
 ):
     part = z.slots // z.load_parts
     head = row_head(z, (z.all_rows, HD))
@@ -128,6 +129,7 @@
 
         return lax.fori_loop(0, z.load_parts, group, (jnp.int32(z.slots),) * R)
 
+    fresh = newest()
     last = sweep(0, score)
     between()
     for r in range(R):
@@ -145,6 +147,7 @@
     msg[:, z.stack :, :] = jnp.zeros((z.n_kv, 8, HD), jnp.float32)
     msg[:, z.stack : z.stack + 1, :] = peaks.reshape(z.n_kv, z.rows, HD).sum(1, keepdims=True)
     msg[:, z.stack + 1 : z.stack + 2, :] = totals.reshape(z.n_kv, z.rows, HD).sum(1, keepdims=True)
+    return fresh
 
 
 def layer(
@@ -185,8 +188,28 @@
             for n in range(4):
                 load_weight(k, n).start()
 
-    attend(
-        z, lens, owner, number, scales, queries, msg, q_rows, kv_buf, qb, s_buf, m_buf, t_buf, n_buf, peak_buf, load, load_weights
+    def newest():
+        factor = 1.0 / math.sqrt(HD)
+        newer = new_ref[...].astype(jnp.float32)
+        small = row_head(z, (z.rows, HD))
+        for a in range(2):
+            for u in range(STEPS):
+                for r in range(R):
+                    pieces = [
+                        jnp.broadcast_to(newer[a, r, u : u + 1, k * HD : (k + 1) * HD], (z.rows, HD))
+                        for k in range(z.kv_heads)
+                    ]
+                    new_x[a, u, r * z.rows : (r + 1) * z.rows, :] = by_head(z, small, pieces)
+        query = q_rows[:, kv].reshape(z.stack, HD)
+        step_of = lax.broadcasted_iota(jnp.int32, (z.stack, 1), 0) % STEPS
+        fresh = [(query * new_x[0, u]).sum(1, keepdims=True) * factor for u in range(STEPS)]
+        fresh = [jnp.where(u <= step_of, fresh[u], very_negative) for u in range(STEPS)]
+        fresh_top = functools.reduce(jnp.maximum, fresh)
+        a_rows[...] = jnp.zeros_like(a_rows)
+        return fresh, fresh_top, step_of
+
+    fresh, fresh_top, step_of = attend(
+        z, lens, owner, number, scales, queries, msg, q_rows, kv_buf, qb, s_buf, m_buf, t_buf, n_buf, peak_buf, load, load_weights, newest
     )
     pl.semaphore_wait(barrier, z.n_kv - 1 + z.n_tp - 1)
 
@@ -201,24 +224,6 @@
         copy = remote(msg.at[there], got.at[d - 1], m_send.at[d - 1], m_recv.at[d - 1], (there, tp))
         copy.start()
         exchange.append(copy)
-
-    factor = 1.0 / math.sqrt(HD)
-    newer = new_ref[...].astype(jnp.float32)
-    small = row_head(z, (z.rows, HD))
-    for a in range(2):
-        for u in range(STEPS):
-            for r in range(R):
-                pieces = [
-                    jnp.broadcast_to(newer[a, r, u : u + 1, k * HD : (k + 1) * HD], (z.rows, HD))
-                    for k in range(z.kv_heads)
-                ]
-                new_x[a, u, r * z.rows : (r + 1) * z.rows, :] = by_head(z, small, pieces)
-    query = q_rows[:, kv].reshape(z.stack, HD)
-    step_of = lax.broadcasted_iota(jnp.int32, (z.stack, 1), 0) % STEPS
-    fresh = [(query * new_x[0, u]).sum(1, keepdims=True) * factor for u in range(STEPS)]
-    fresh = [jnp.where(u <= step_of, fresh[u], very_negative) for u in range(STEPS)]
-    fresh_top = functools.reduce(jnp.maximum, fresh)
-    a_rows[...] = jnp.zeros_like(a_rows)
 
     for copy in exchange:
         copy.wait_recv()
@@ -285,50 +290,71 @@
             put(slice(0, z.half), first[0:8])
             put(slice(z.half, 2 * z.half), first[8:16])
 
-    paired = []
-    for i, e in enumerate(turns):
-        for n, d in enumerate(order):
-
-            def put(where, value):
-                sent1[i, n, :, where] = value
-
-            fill(2 * flip(high, d) + 1 - side, (tp + e) % z.n_tp, put)
-        copy = remote(sent1.at[i], got1.at[i], send1.at[i], recv1.at[i], (partner, tp))
+    paired, spread, last, totals = [], [], [], []
+    groups = z.groups
+    firsts = [sum(groups[:i]) for i in range(len(groups))]
+
+    def pair_step(i):
+        for m in range(firsts[i], firsts[i] + groups[i]):
+            for n, d in enumerate(order):
+
+                def put(where, value):
+                    sent1[m, n, :, where] = value
+
+                fill(2 * flip(high, d) + 1 - side, (tp + turns[m]) % z.n_tp, put)
+        piece = pl.ds(firsts[i], groups[i])
+        copy = remote(sent1.at[piece], got1.at[piece], send1.at[i], recv1.at[i], (partner, tp))
         copy.start()
         paired.append(copy)
 
-    spread = []
-    for i, e in enumerate(turns):
+    def spread_step(i):
         paired[i].wait_recv()
+        piece = pl.ds(firsts[i], groups[i])
         arriving = []
         for n, d in enumerate(order):
-
-            def put(where, value):
-                sent2[i, n, :, where] = value + got1[i, n, :, where]
-
             there = 2 * flip(high, d) + side
-            fill(there, (tp + e) % z.n_tp, put)
+            for m in range(firsts[i], firsts[i] + groups[i]):
+
+                def put(where, value):
+                    sent2[n, m, :, where] = value + got1[m, n, :, where]
+
+                fill(there, (tp + turns[m]) % z.n_tp, put)
             if d > 0:
                 copy = remote(
-                    sent2.at[i, n], got2.at[i, d - 1], send2.at[i, d - 1], recv2.at[i, d - 1], (there, tp)
+                    sent2.at[n, piece], got2.at[d - 1, piece], send2.at[i, d - 1], recv2.at[i, d - 1], (there, tp)
                 )
                 copy.start()
                 arriving.append(copy)
         spread.append(arriving)
 
-    last = []
-    for i, e in enumerate(turns):
+    def last_step(i):
         for copy in spread[i]:
             copy.wait_recv()
-        value = sent2[i, z.pairs - 1]
-        for d in range(z.pairs - 1):
-            value = value + got2[i, d]
-        if e > 0:
-            sums[e - 1] = value
-            there = (tp + e) % z.n_tp
-            copy = remote(sums.at[e - 1], got3.at[e - 1], send3.at[e - 1], recv3.at[e - 1], (kv, there))
-            copy.start()
-            last.append(copy)
+        for m in range(firsts[i], firsts[i] + groups[i]):
+            e = turns[m]
+            value = sent2[z.pairs - 1, m]
+            for d in range(z.pairs - 1):
+                value = value + got2[d, m]
+            totals.append(value)
+            if e > 0:
+                sums[e - 1] = value
+                there = (tp + e) % z.n_tp
+                copy = remote(sums.at[e - 1], got3.at[e - 1], send3.at[e - 1], recv3.at[e - 1], (kv, there))
+                copy.start()
+                last.append(copy)
+
+    ahead, lag = 2, 2
+    for i in range(min(ahead, len(groups))):
+        pair_step(i)
+    for i in range(len(groups)):
+        spread_step(i)
+        if i + ahead < len(groups):
+            pair_step(i + ahead)
+        if i >= lag:
+            last_step(i - lag)
+    for i in range(max(len(groups) - lag, 0), len(groups)):
+        last_step(i)
+    value = totals[-1]
     for copy in last:
         copy.wait_recv()
     for e in range(z.n_tp - 1):
@@ -373,8 +399,8 @@
         pltpu.VMEM((2, 16, z.kv_heads * z.inner), f32),
         pltpu.VMEM((z.n_tp, z.pairs, *part), f32),
         pltpu.VMEM((z.n_tp, z.pairs, *part), f32),
-        pltpu.VMEM((z.n_tp, z.pairs, *part), f32),
-        pltpu.VMEM((z.n_tp, rest, *part), f32),
+        pltpu.VMEM((z.pairs, z.n_tp, *part), f32),
+        pltpu.VMEM((rest, z.n_tp, *part), f32),
         pltpu.VMEM((others, *part), f32),
         pltpu.VMEM((others, *part), f32),
         pltpu.VMEM((16, z.cols), f32),
@@ -382,10 +408,10 @@
         dma((z.kv_heads, 4)),
         dma((z.n_kv - 1,)),
         dma((z.n_kv - 1,)),
-        dma((z.n_tp,)),
-        dma((z.n_tp,)),
-        dma((z.n_tp, rest)),
-        dma((z.n_tp, rest)),
+        dma((len(z.groups),)),
+        dma((len(z.groups),)),
+        dma((len(z.groups), rest)),
+        dma((len(z.groups), rest)),
         dma((others,)),
         dma((others,)),
     ]

time: 26.3 us -> 26 us (0.989)
  Pallas kernels: 24.8 us -> 24.5 us
    pallas_call x1, Pallas kernels: 24.8 us -> 24.5 us  [shards(): pl.pallas_call(functools.partial(layer, z), out_shape=jax.ShapeDtypeStruc...]
where the time goes in v3:
time: 26 us; the launch traced here: 25.8 us
  Pallas kernels  24.5 us (94%)
  other arithmetic  1.35 us (5%)
    pallas_call x1, Pallas kernels, shards(): pl.pallas_call(functools.partial(layer, z), out_shape=jax.ShapeDtypeStruc...  24.5 us
    convert_element_type x1, other arithmetic, shards(): return out.transpose(1, 0, 2).astype(jnp.bfloat16)  1.35 us

profile of v3, /device:TPU:0, one launch (start us, length us, event | category | flops | bytes accessed | tf_op | source)
XLA Modules:
  0.0 25.8 jit_solution(8859577999920121590)
XLA Ops:
  0.0 24.5 %layer.1 = f32[6,2,512]{2,1,0:T(2,128)} custom-call(s32[6]{0:T(128)} %lens.1, s32[32]{0:T(128)} %owner.1, s32[32]{0:T(128)} %number.1, f32[2,2,32]{2,1,0:T(2,128)} %bitcast.7, bf16[6,2,4096]{2,1,0:T(2,128)(2,1)} %bitcast.5, bf16[2,6,2,256]{3,2,1,0:T(2,128)(2,1)} %bitcast.6, bf16[2,32,256,256]{3,2,1,0:T(8,128)(2,1)} %cache.1, bf16[2,256,16384]{2,1,0:T(8,128)(2,1)} %w_ref.1), custom_call_target="tpu_custom_call" | custom-call | tf_op jit(solution)/shard_map/layer/pallas_call | solution.py:431
  24.5 1.3 %convert_bitcast_fusion = bf16[2,6,512]{2,0,1:T(2,128)(2,1)} fusion(f32[6,2,512]{2,1,0:T(2,128)} %layer.1), kind=kLoop, calls=%fused_computation | loop fusion | flops 6144 | bytes 36864 | tf_op jit(solution)/shard_map/convert_element_type | solution.py:451

commit v4 on v3

--- a/solution.py
+++ b/solution.py
@@ -368,8 +368,8 @@
         whole[0:8, :] = value[:, : z.half]
         whole[8:16, :] = value[:, z.half :]
     for r in range(R):
-        for s in range(STEPS):
-            out_ref[r, s : s + 1, :] = whole[s * R + r : s * R + r + 1, :]
+        rows = [whole[s * R + r : s * R + r + 1, :] for s in range(STEPS)]
+        out_ref[r] = jnp.concatenate(rows, 0).astype(jnp.bfloat16)
     for copy in exchange:
         copy.wait_send()
     for copy in paired + sum(spread, []) + last:
@@ -430,7 +430,7 @@
     z = Sizes(n_kv, n_tp, kv_heads, kv_cache.shape[1], out_weight.shape[2])
     out = pl.pallas_call(
         functools.partial(layer, z),
-        out_shape=jax.ShapeDtypeStruct((R, STEPS, z.cols), jnp.float32),
+        out_shape=jax.ShapeDtypeStruct((R, STEPS, z.cols), jnp.bfloat16),
         in_specs=spaces(*"ssssvvhh"),
         out_specs=spaces("v")[0],
         scratch_shapes=scratch(z),
@@ -448,7 +448,7 @@
         kv_cache,
         out_weight,
     )
-    return out.transpose(1, 0, 2).astype(jnp.bfloat16)
+    return out.transpose(1, 0, 2)
 
 
 def solution(mesh):

time: 26 us -> 26 us (level)
  other arithmetic: 1.35 us -> 0 us
  local copies, waits for them, and re-layouts: 0 us -> 1.32 us
    convert_element_type x1 -> x0, other arithmetic: 1.35 us -> none  [shards(): return out.transpose(1, 0, 2).astype(jnp.bfloat16)]
    unnamed x0 -> x1, local copies, waits for them, and re-layouts: none -> 1.32 us
where the time goes in v4:
time: 26 us; the launch traced here: 25.8 us
  Pallas kernels  24.5 us (94%)
  local copies, waits for them, and re-layouts  1.32 us (5%)
    pallas_call x1, Pallas kernels, shards(): pl.pallas_call(functools.partial(layer, z), out_shape=jax.ShapeDtypeStruc...  24.5 us
    unnamed x1, local copies, waits for them, and re-layouts  1.32 us

profile of v4, /device:TPU:0, one launch (start us, length us, event | category | flops | bytes accessed | tf_op | source)
XLA Modules:
  0.0 25.8 jit_solution(6357785544919166447)
XLA Ops:
  0.0 24.5 %layer.1 = bf16[6,2,512]{2,1,0:T(2,128)(2,1)} custom-call(s32[6]{0:T(128)} %lens.1, s32[32]{0:T(128)} %owner.1, s32[32]{0:T(128)} %number.1, f32[2,2,32]{2,1,0:T(2,128)} %bitcast.7, bf16[6,2,4096]{2,1,0:T(2,128)(2,1)} %bitcast.4, bf16[2,6,2,256]{3,2,1,0:T(2,128)(2,1)} %bitcast.6, bf16[2,32,256,256]{3,2,1,0:T(8,128)(2,1)} %cache.1, bf16[2,256,16384]{2,1,0:T(8,128)(2,1)} %w_ref.1), custom_call_target="tpu_custom_call" | custom-call | tf_op jit(solution)/shard_map/layer/pallas_call | solution.py:431
  24.5 1.3 %copy.10 = bf16[2,6,512]{2,0,1:T(2,128)(2,1)} copy(bf16[2,6,512]{2,0,1:T(2,128)(2,1)} %bitcast.5) | data formatting | bytes 24576
